TPU v7x, 128 devices: a whole 4x4x4 slice. The times are simulated.
128 devices in a mesh: pas: 32 (over y, z, core), tp: 4 (over x).
Axes of the slice: x: 4, y: 4, z: 4, core: 2. Of those that a mesh axis runs over, the one named last changes fastest.
Arguments:
- passage_hidden: bfloat16 [32768, 8192], P('pas', 'tp'), may hold values from -6 to 6
- kv_weight: bfloat16 [1024, 8192], P('pas', 'tp'), may hold values from -0.0625 to 0.0625
- queries: bfloat16 [16384, 4096], P('pas', 'tp'), may hold values from -600 to 600
- query_kv: bfloat16 [16384, 1024], P('pas', 'tp'), may hold values from -6 to 6
- out_grad: bfloat16 [16384, 4096], P('pas', 'tp'), may hold values from -6 to 6
- source_device: int32 [128, 8], P('pas'), may hold values from 0 to 31, all different within a row; in each aligned block of 4 rows (0 to 3, 4 to 7, ...) at most 2 rows name the same one
- source_slot: int32 [128, 8], P('pas'), may hold values from 0 to 7
Outputs:
- query_grad: bfloat16 [16384, 4096], P('pas', 'tp')
- query_kv_grad: bfloat16 [16384, 1024], P('pas', 'tp')
- weight_grad: float32 [1024, 8192], P('pas', 'tp')
Inputs may be any that keep to these rules, and one draw needn't show every extreme that they name: `source_device`: each query names 8 different owners; among the 4 queries of one index of pas no owner is named more than 2 times, and one owner exactly 2 times.
All inputs are finite; a program needn't handle non-finite values.
Results may differ from a plain program's by a relative error of at most 0.0095.
Values may be sent and summed in bfloat16 or wider, within the bound.
No kernel may reach another device: no remote copies, remote signals or barrier semaphores. Data moves between devices by JAX's collectives and lax.ppermute only.
A program may use at most 128 MiB of HBM per device.

v0:
```python
import jax
import jax.numpy as jnp
from jax import lax
from jax.sharding import PartitionSpec as P

HD = 128
PLEN = 128


def attend_block(query_rows, keys_values, grad_out, prefix):
    query_len = query_rows.shape[0]
    key_len = keys_values.shape[0]
    kv_heads = keys_values.shape[1] // (2 * HD)
    group_size = query_rows.shape[1] // (HD * kv_heads)
    paired = keys_values.reshape(key_len, kv_heads, 2, HD)
    key_heads = paired[:, :, 0, :]
    value_heads = paired[:, :, 1, :]
    query_heads = query_rows.reshape(query_len, kv_heads, group_size, HD)
    grad_heads = grad_out.reshape(query_len, kv_heads, group_size, HD)
    scaling = HD ** (-0.5)
    scores = (
        jnp.einsum("qhgd,khd->hgqk", query_heads, key_heads, preferred_element_type=jnp.float32)
        * scaling
    )
    row_index = jnp.arange(query_len)[:, None]
    col_index = jnp.arange(key_len)[None, :]
    visible = jnp.logical_or(col_index < prefix, col_index - prefix <= row_index)
    scores = jnp.where(visible, scores, jnp.float32(-1e30))
    largest = jnp.max(scores, axis=-1, keepdims=True)
    exponent = jnp.exp(scores - largest)
    weights = exponent / jnp.sum(exponent, axis=-1, keepdims=True)
    weights_low = weights.astype(jnp.bfloat16)
    outputs = jnp.einsum(
        "hgqk,khd->hgqd", weights_low, value_heads, preferred_element_type=jnp.float32
    )
    grad_float = grad_heads.astype(jnp.float32).transpose(1, 2, 0, 3)
    delta_rows = jnp.sum(outputs * grad_float, axis=-1, keepdims=True)
    grad_weights = jnp.einsum(
        "qhgd,khd->hgqk", grad_heads, value_heads, preferred_element_type=jnp.float32
    )
    grad_low = (weights * (grad_weights - delta_rows)).astype(jnp.bfloat16)
    grad_query = (
        jnp.einsum("hgqk,khd->qhgd", grad_low, key_heads, preferred_element_type=jnp.float32)
        * scaling
    )
    grad_query = grad_query.astype(jnp.bfloat16).reshape(query_len, kv_heads * group_size * HD)
    grad_keys = (
        jnp.einsum("hgqk,qhgd->khd", grad_low, query_heads, preferred_element_type=jnp.float32)
        * scaling
    )
    grad_values = jnp.einsum(
        "hgqk,qhgd->khd", weights_low, grad_heads, preferred_element_type=jnp.float32
    )
    grad_pairs = jnp.stack([grad_keys, grad_values], axis=2).reshape(key_len, kv_heads * 2 * HD)
    return (grad_query, grad_pairs)


def per_device(passage_hidden, kv_weight, queries, query_kv, out_grad, source_device, source_slot):
    owners = lax.axis_size("pas")
    rows_local = passage_hidden.shape[0]
    local_width = query_kv.shape[1]
    passages_here = rows_local // PLEN
    queries_here = source_device.shape[0]
    retrieved = source_device.shape[1]
    requests_total = queries_here * retrieved
    capacity = min(queries_here, max(2, 2 * requests_total // owners))
    query_length = queries.shape[0] // queries_here
    partial_kv = jnp.einsum(
        "rd,cd->rc",
        passage_hidden,
        lax.all_gather(kv_weight, "pas", axis=0, tiled=True),
        preferred_element_type=jnp.float32,
    )
    passage_kv = lax.psum_scatter(partial_kv, "tp", scatter_dimension=1, tiled=True).astype(
        jnp.bfloat16
    )
    passage_kv = passage_kv.reshape(passages_here, PLEN, local_width)
    flat_device = source_device.reshape(-1)
    flat_slot = source_slot.reshape(-1)
    owner_hits = (flat_device[:, None] == jnp.arange(owners, dtype=jnp.int32)[None, :]).astype(
        jnp.int32
    )
    earlier = jnp.cumsum(owner_hits, axis=0) - owner_hits
    ranking = jnp.sum(owner_hits * earlier, axis=1)
    slot_hits = (ranking[:, None] == jnp.arange(capacity, dtype=jnp.int32)[None, :]).astype(
        jnp.int32
    )
    placed = owner_hits[:, :, None] * slot_hits[:, None, :]
    request_table = jnp.sum(placed * (flat_slot + 1)[:, None, None], axis=0) - 1
    wanted = lax.all_to_all(request_table, "pas", split_axis=0, concat_axis=0, tiled=True)
    global_ids = flat_device * passages_here + flat_slot
    initial = jnp.zeros((requests_total, PLEN, local_width), jnp.bfloat16)
    piece_rows = lax.all_gather(passage_kv, "pas", axis=0, tiled=True)
    inside = jnp.logical_and(global_ids >= 0, global_ids < piece_rows.shape[0])
    taken_rows = piece_rows[jnp.clip(global_ids, 0, piece_rows.shape[0] - 1)]
    fetched = jnp.where(inside[:, None, None], taken_rows, initial)
    remote_rows = retrieved * PLEN

    def one_query(inputs):
        query_rows, own_pairs, grad_out, remote_pairs = inputs
        keys_values = jnp.concatenate([remote_pairs, own_pairs], axis=0)
        grad_query, grad_pairs = attend_block(query_rows, keys_values, grad_out, remote_rows)
        return (
            grad_query,
            grad_pairs[:remote_rows].astype(jnp.bfloat16),
            grad_pairs[remote_rows:].astype(jnp.bfloat16),
        )

    grad_queries, remote_grads, own_grads = lax.map(
        one_query,
        (
            queries.reshape(queries_here, query_length, queries.shape[1]),
            query_kv.reshape(queries_here, query_length, local_width),
            out_grad.reshape(queries_here, query_length, out_grad.shape[1]),
            fetched.reshape(queries_here, remote_rows, local_width),
        ),
    )
    outgoing_grads = jnp.zeros((owners, capacity, PLEN, local_width), jnp.bfloat16)
    outgoing_grads = outgoing_grads.at[flat_device, ranking].set(
        remote_grads.reshape(requests_total, PLEN, local_width)
    )
    returned = lax.all_to_all(outgoing_grads, "pas", split_axis=0, concat_axis=0, tiled=True)
    slot_select = (
        wanted[:, :, None] == jnp.arange(passages_here, dtype=jnp.int32)[None, None, :]
    ).astype(jnp.bfloat16)
    grad_total = jnp.einsum(
        "ncs,ncpk->spk", slot_select, returned, preferred_element_type=jnp.float32
    )
    grad_kv = grad_total.astype(jnp.bfloat16).reshape(rows_local, local_width)
    full_grad = lax.all_gather(grad_kv, "tp", axis=1, tiled=True)
    weight_grad = lax.psum_scatter(
        jnp.einsum("rc,rd->cd", full_grad, passage_hidden, preferred_element_type=jnp.float32),
        "pas",
        scatter_dimension=0,
        tiled=True,
    )
    return (
        grad_queries.reshape(queries_here * query_length, queries.shape[1]),
        own_grads.reshape(queries_here * query_length, local_width),
        weight_grad,
    )


def solution(mesh):
    in_specs = (
        P("pas", "tp"),
        P("pas", "tp"),
        P("pas", "tp"),
        P("pas", "tp"),
        P("pas", "tp"),
        P("pas", None),
        P("pas", None),
    )
    out_specs = (P("pas", "tp"), P("pas", "tp"), P("pas", "tp"))
    return jax.shard_map(
        per_device, mesh=mesh, in_specs=in_specs, out_specs=out_specs, check_vma=False
    )
```

profile of v0, /device:TPU:0, one launch (start us, length us, event | category | flops | bytes accessed | tf_op | source)
XLA Modules:
  0.0 483.3 jit_solution(6588597384418245049)
XLA Ops:
  7.9 51.2 %all-gather.4.cloned.1.call-done = bf16[1024,2048]{1,0:T(8,128)(2,1)} async-done(((bf16[32,2048]{1,0:T(8,128)(2,1)}), bf16[1024,2048]{1,0:T(8,128)(2,1)}) %all-gather.4.cloned.1.call-update) | async-done | bytes 4194320 | tf_op jit(solution)/shard_map/all_gather | solution.py:71
  59.2 9.9 %fusion.49 = f32[1024,1024]{1,0:T(8,128)} fusion(bf16[1024,2048]{1,0:T(8,128)(2,1)} %param.9, bf16[1024,2048]{1,0:T(8,128)(2,1)} %all-gather.4.cloned.1.call-done), kind=kOutput, calls=%fused_computation.76 | convolution fusion | flops 4294967296 | bytes 12582912 | tf_op jit(solution)/shard_map/rd,cd->rc/dot_general | solution.py:68
  69.2 46.2 %reduce-scatter.3.cloned.1.call-done = f32[1024,256]{1,0:T(8,128)} async-done(((f32[1024,1024]{1,0:T(8,128)}), f32[1024,256]{1,0:T(8,128)}) %reduce-scatter.3.cloned.1.call-update) | async-done | bytes 1048592 | tf_op jit(solution)/shard_map/reduce_scatter | solution.py:74
  115.3 2.1 convert_element_type.88
  118.8 7.4 %all-to-all-start = ((s32[32,1,2]{2,1,0:T(1,128)}), s32[32,1,2]{2,1,0:T(1,128)S(1)}, u32[]{:S(2)}, u32[]{:S(2)}) async-start(s32[32,1,2]{2,1,0:T(1,128)} %copy.97), calls=%async_computation.1 | async-start | bytes 32768 | tf_op jit(solution)/shard_map/all_to_all | solution.py:90
  126.5 64.3 %all-gather.6.cloned.1.call-done = bf16[256,128,256]{2,1,0:T(8,128)(2,1)} async-done(((bf16[8,128,256]{2,1,0:T(8,128)(2,1)}), bf16[256,128,256]{2,1,0:T(8,128)(2,1)}) %all-gather.6.cloned.1.call-update) | async-done | bytes 16777232 | tf_op jit(solution)/shard_map/all_gather | solution.py:93
  190.8 6.4 %gather_fusion = bf16[32,128,256]{2,1,0:T(8,128)(2,1)S(1)} fusion(bf16[256,128,256]{2,1,0:T(8,128)(2,1)} %all-gather.6.cloned.1.call-done, s32[1024]{0:T(1024)S(1)} %pad_clamp_fusion), kind=kCustom, calls=%fused_computation | custom fusion | bytes 4194432 | tf_op jit(solution)/shard_map/gather | solution.py:95
  197.3 1.7 bitcast_select_fusion.1
  199.0 56.9 %while.17 = (s32[]{:T(128)}, bf16[4,128,1024]{2,1,0:T(8,128)(2,1)S(1)}, bf16[4,1024,256]{2,1,0:T(8,128)(2,1)}, bf16[4,128,256]{2,1,0:T(8,128)(2,1)}, bf16[4,1024...) while((s32[]{:T(128)}, ...), condition=%wide.region_5.6_spmd.clone, body=%wide.region_1.5_spmd.sunk.clone | while | flops 1839561984 | bytes 48061812 | solution.py:109
  200.1 0.9 fusion.108
  201.0 1.1 constant_dynamic-slice_fusion.12
  202.6 1.1 constant_dynamic-slice_fusion.10
  205.6 1.2 fusion.111
  206.9 1.3 convolution_bitcast_fusion.4
  208.2 1.5 fusion.112
  210.2 0.9 fusion.114
  214.3 0.9 fusion.108
  215.2 1.1 constant_dynamic-slice_fusion.12
  216.8 1.1 constant_dynamic-slice_fusion.10
  219.8 1.2 fusion.111
  221.1 1.3 convolution_bitcast_fusion.4
  222.4 1.5 fusion.112
  224.4 0.9 fusion.114
  228.5 0.9 fusion.108
  229.4 1.1 constant_dynamic-slice_fusion.12
  231.0 1.1 constant_dynamic-slice_fusion.10
  234.0 1.2 fusion.111
  235.3 1.3 convolution_bitcast_fusion.4
  236.6 1.5 fusion.112
  238.6 0.9 fusion.114
  242.7 0.9 fusion.108
  243.6 1.1 constant_dynamic-slice_fusion.12
  245.2 1.1 constant_dynamic-slice_fusion.10
  248.3 1.2 fusion.111
  249.5 1.3 convolution_bitcast_fusion.4
  250.8 1.5 fusion.112
  252.8 0.9 fusion.114
  255.0 0.9 constant_dynamic-update-slice_fusion.10
  255.9 2.5 broadcast_in_dim.73
  259.0 5.8 %scatter_fusion = bf16[32,2,128,256]{3,2,1,0:T(8,128)(2,1)} fusion(bf16[32,2,128,256]{3,2,1,0:T(8,128)(2,1)} %broadcast_in_dim.73, s32[32]{0:T(128)S(1)} %get-tuple-element.161, bf16[32,128,256]{2,1,0:T(8,128)(2,1)S(1)} %bitcast.256), kind=kCustom, calls=%fused_computation.1 | custom fusion | bytes 6291712 | tf_op jit(solution)/shard_map/scatter | solution.py:119
  264.8 8.5 %copy.100 = bf16[32,2,128,256]{3,1,2,0:T(2,128)(2,1)} copy(bf16[32,2,128,256]{3,2,1,0:T(8,128)(2,1)} %scatter_fusion) | data formatting | bytes 8388608 | tf_op jit(solution)/shard_map/scatter | solution.py:119
  273.3 5.5 %all-to-all-start.1 = ((bf16[32,2,128,256]{3,1,2,0:T(2,128)(2,1)}), bf16[32,2,128,256]{3,1,2,0:T(2,128)(2,1)}, u32[]{:S(2)}, u32[]{:S(2)}) async-start(bf16[32,2,128,256]{3,1,2,0:T(2,128)(2,1)} %copy.100), calls=%async_computation.2 | async-start | bytes 8388608 | tf_op jit(solution)/shard_map/all_to_all | solution.py:122
  279.0 52.6 %all-to-all-done.1 = bf16[32,2,128,256]{3,1,2,0:T(2,128)(2,1)} async-done(((bf16[32,2,128,256]{3,1,2,0:T(2,128)(2,1)}), bf16[32,2,128,256]{3,1,2,0:T(2,128)(2,1)}, u32[]{:S(2)}, u32[]{:S(2)}) %all-to-all-start.1) | async-done | bytes 4194336 | tf_op jit(solution)/shard_map/all_to_all | solution.py:122
  331.6 4.5 fusion.39
  336.1 0.9 copy.102
  337.1 35.0 %all-gather.8.cloned.1.call-done = bf16[1024,1024]{1,0:T(8,128)(2,1)} async-done(((bf16[1024,256]{1,0:T(8,128)(2,1)}), bf16[1024,1024]{1,0:T(8,128)(2,1)}) %all-gather.8.cloned.1.call-update) | async-done | bytes 2097168 | tf_op jit(solution)/shard_map/all_gather | solution.py:130
  372.1 10.6 %fusion.50 = f32[1024,2048]{1,0:T(8,128)} fusion(bf16[1024,1024]{1,0:T(8,128)(2,1)} %all-gather.8.cloned.1.call-done, bf16[1024,2048]{1,0:T(8,128)(2,1)} %param.9), kind=kOutput, calls=%fused_computation.77 | convolution fusion | flops 4294967296 | bytes 14680064 | tf_op jit(solution)/shard_map/rc,rd->cd/dot_general | solution.py:132
  382.8 94.0 %reduce-scatter.5.cloned.1.call-done = f32[32,2048]{1,0:T(8,128)} async-done(((f32[1024,2048]{1,0:T(8,128)}), f32[32,2048]{1,0:T(8,128)}) %reduce-scatter.5.cloned.1.call-update) | async-done | bytes 262160 | tf_op jit(solution)/shard_map/reduce_scatter | solution.py:131
  (123 shorter events, 27.0 us)
Async XLA Ops:
  7.2 52.0 %all-gather.4.cloned.1.call-start = ((), (), s32[]{:S(2)}) async-start(), calls=%async_computation.4 | async-start | bytes 4325376 | tf_op jit(solution)/shard_map/all_gather | solution.py:71
  7.9 107.4 %reduce-scatter.3.cloned.1.call-start = ((), (), s32[]{:S(2)}) async-start(), calls=%async_computation.5 | async-start | bytes 5242880 | tf_op jit(solution)/shard_map/reduce_scatter | solution.py:74
  69.1 48.3 %copy-start.2 = (s32[4,8]{1,0:T(4,128)S(1)}, s32[4,8]{1,0:T(4,128)}, u32[]{:S(2)}) copy-start(s32[4,8]{1,0:T(4,128)} %param.14) | copy-start | bytes 388
  69.1 48.4 %copy-start.1 = (s32[4,8]{1,0:T(4,128)S(1)}, s32[4,8]{1,0:T(4,128)}, u32[]{:S(2)}) copy-start(s32[4,8]{1,0:T(4,128)} %param.15) | copy-start | bytes 388
  69.1 121.7 %all-gather.6.cloned.1.call-start = ((), (), s32[]{:S(2)}) async-start(), calls=%async_computation.6 | async-start | bytes 17301504 | tf_op jit(solution)/shard_map/all_gather | solution.py:93
  118.8 154.6 %all-to-all-start = ((s32[32,1,2]{2,1,0:T(1,128)}), s32[32,1,2]{2,1,0:T(1,128)S(1)}, u32[]{:S(2)}, u32[]{:S(2)}) async-start(s32[32,1,2]{2,1,0:T(1,128)} %copy.97), calls=%async_computation.1 | async-start | bytes 32768 | tf_op jit(solution)/shard_map/all_to_all | solution.py:90
  255.9 8.9 %copy-start.3 = (bf16[4,128,1024]{2,1,0:T(8,128)(2,1)}, bf16[4,128,1024]{2,1,0:T(8,128)(2,1)S(1)}, u32[]{:S(2)}) copy-start(bf16[4,128,1024]{2,1,0:T(8,128)(2,1)S(1)} %get-tuple-element.106) | copy-start | bytes 3145732
  255.9 3.2 copy-start
  273.3 58.3 %all-to-all-start.1 = ((bf16[32,2,128,256]{3,1,2,0:T(2,128)(2,1)}), bf16[32,2,128,256]{3,1,2,0:T(2,128)(2,1)}, u32[]{:S(2)}, u32[]{:S(2)}) async-start(bf16[32,2,128,256]{3,1,2,0:T(2,128)(2,1)} %copy.100), calls=%async_computation.2 | async-start | bytes 8388608 | tf_op jit(solution)/shard_map/all_to_all | solution.py:122
  278.9 93.3 %all-gather.8.cloned.1.call-start = ((), (), s32[]{:S(2)}) async-start(), calls=%async_computation.7 | async-start | bytes 2621440 | tf_op jit(solution)/shard_map/all_gather | solution.py:130
  337.0 139.7 %reduce-scatter.5.cloned.1.call-start = ((), (), s32[]{:S(2)}) async-start(), calls=%async_computation.8 | async-start | bytes 8650752 | tf_op jit(solution)/shard_map/reduce_scatter | solution.py:131
Sparse Core Ops, SparseCore 0:
  10.3 48.8 all-gather.3
  69.3 46.0 reduce-scatter.2
  118.4 72.3 all-gather.5
  337.2 34.9 all-gather.7
  382.9 93.8 reduce-scatter.4
where the time goes:
time: 484 us; the launch traced here: 483 us
  waiting for transfers between devices  344 us (71%)
  local copies, waits for them, and re-layouts  50.2 us (10%)
  matrix products  50 us (10%)
  between operations  13.9 us (3%)
  starting transfers between devices  13.1 us (3%)
  other arithmetic  11.3 us (2%)
    reduce_scatter x1, waiting for transfers between devices, per_device(): lax.psum_scatter(jnp.einsum('rc,rd->cd', full_grad, passage_hidden, prefe...  94 us
    all_gather x1, waiting for transfers between devices, per_device(): piece_rows = lax.all_gather(passage_kv, 'pas', axis=0, tiled=True)  64.3 us
    all_to_all x1, waiting for transfers between devices, per_device(): lax.all_to_all(outgoing_grads, 'pas', split_axis=0, concat_axis=0, tiled=...  52.6 us
    all_gather x1, waiting for transfers between devices, per_device(): lax.all_gather(kv_weight, 'pas', axis=0, tiled=True)  51.2 us
    reduce_scatter x1, waiting for transfers between devices, per_device(): lax.psum_scatter(partial_kv, 'tp', scatter_dimension=1, tiled=True)  46.2 us
    all_gather x1, waiting for transfers between devices, per_device(): full_grad = lax.all_gather(grad_kv, 'tp', axis=1, tiled=True)  35 us
    dynamic_slice x28, local copies, waits for them, and re-layouts, per_device(): lax.map(one_query, (queries.reshape(queries_here, query_length, queries.s...  14.6 us
    scatter x2, local copies, waits for them, and re-layouts, per_device(): outgoing_grads.at[flat_device, ranking]  14.3 us
  transfers between devices with their start and end apart: 7, of which 6 were waited for; matrix products, arithmetic and copies ran while one was open for 17% of the time, Pallas kernels for 0%

commit v1 on v0

v1 whole, which is shorter than its diff:
```python
import functools
import math

import jax
import jax.numpy as jnp
from jax import lax
from jax.experimental import pallas as pl
from jax.experimental.pallas import tpu as pltpu
from jax.sharding import PartitionSpec as P

HD = 128
PLEN = 128
BF = jnp.bfloat16
F32 = jnp.float32
NT = (((1,), (1,)), ((), ()))
TN = (((0,), (0,)), ((), ()))


def attention_kernel(
    n_src, src_buf, src_row, dst_row, q_ref, do_ref, own_ref, *rest
):
    srcs = rest[:n_src]
    dq_ref, down_ref, out_ref = rest[n_src : n_src + 3]
    kv, stage, q_st, do_st, p_t, ds_t, in_sem, out_sem = rest[n_src + 3 :]
    step = pl.program_id(0)
    steps = pl.num_programs(0)
    group = q_ref.shape[1] // HD
    retrieved = in_sem.shape[1]
    rows = retrieved * PLEN
    keys = rows + own_ref.shape[0]
    slot = lax.rem(step, 2)
    scaling = HD ** (-0.5)

    def fetch(query, into):
        for j in range(retrieved):
            at = query * retrieved + j
            for b in range(n_src):

                @pl.when(src_buf[at] == b)
                def _():
                    pltpu.make_async_copy(
                        srcs[b].at[src_row[at]],
                        kv.at[into, pl.ds(j * PLEN, PLEN)],
                        in_sem.at[into, j],
                    ).start()

    @pl.when(step == 0)
    def _():
        fetch(0, 0)

    @pl.when(step + 1 < steps)
    def _():
        fetch(step + 1, 1 - slot)

    for g in range(group):
        q_st[pl.ds(g * HD, HD), :] = q_ref[:, g * HD : (g + 1) * HD]
        do_st[pl.ds(g * HD, HD), :] = do_ref[:, g * HD : (g + 1) * HD]
    kv[slot, pl.ds(rows, keys - rows), :] = own_ref[...]
    for j in range(retrieved):
        pltpu.make_async_copy(
            srcs[0].at[0], kv.at[slot, pl.ds(j * PLEN, PLEN)], in_sem.at[slot, j]
        ).wait()

    k_all = kv[slot, :, :HD]
    v_all = kv[slot, :, HD:]
    width = 2 * HD
    key_at = lax.broadcasted_iota(jnp.int32, (keys - rows, width), 0)
    tok_at = lax.broadcasted_iota(jnp.int32, (keys - rows, width), 1) % HD
    visible = key_at <= tok_at
    for g in range(0, group, 2):
        cols = pl.ds(g * HD, width)
        s = lax.dot_general(k_all, q_st[cols, :], NT, preferred_element_type=F32)
        s = jnp.concatenate(
            [s[:rows], jnp.where(visible, s[rows:], F32(-1e30))], axis=0
        )
        largest = jnp.max(s, axis=0, keepdims=True)
        e = jnp.exp2((s - largest) * F32(scaling * math.log2(math.e)))
        w = e * (1.0 / jnp.sum(e, axis=0, keepdims=True))
        w_low = w.astype(BF)
        p_t[:, cols] = w_low
        gw = lax.dot_general(v_all, do_st[cols, :], NT, preferred_element_type=F32)
        delta = jnp.sum(w_low.astype(F32) * gw, axis=0, keepdims=True)
        ds_t[:, cols] = (w * (gw - delta)).astype(BF)
    d_v = jnp.dot(p_t[...], do_st[...], preferred_element_type=F32)
    d_k = jnp.dot(ds_t[...], q_st[...], preferred_element_type=F32) * F32(scaling)
    dq_t = lax.dot_general(k_all, ds_t[...], TN, preferred_element_type=F32) * F32(scaling)
    for g in range(group):
        dq_ref[:, g * HD : (g + 1) * HD] = dq_t[:, g * HD : (g + 1) * HD].T.astype(BF)

    down_ref[:, :HD] = d_k[rows:].astype(BF)
    down_ref[:, HD:] = d_v[rows:].astype(BF)

    def sent(query, at_slot, j):
        return pltpu.make_async_copy(
            stage.at[at_slot, pl.ds(j * PLEN, PLEN)],
            out_ref.at[dst_row[query * retrieved + j]],
            out_sem.at[at_slot, j],
        )

    @pl.when(step >= 2)
    def _():
        for j in range(retrieved):
            sent(step - 2, slot, j).wait()

    stage[slot, :, :HD] = d_k[:rows].astype(BF)
    stage[slot, :, HD:] = d_v[:rows].astype(BF)
    for j in range(retrieved):
        sent(step, slot, j).start()

    @pl.when(step == steps - 1)
    def _():
        for j in range(retrieved):
            if steps > 1:
                sent(step - 1, 1 - slot, j).wait()
            sent(step, slot, j).wait()


def attention(queries, out_grad, query_kv, sources, src_buf, src_row, dst_row, slots, n_query):
    rows, width = queries.shape
    qlen = rows // n_query
    retrieved = src_buf.shape[0] // n_query
    keys = retrieved * PLEN + qlen
    local = query_kv.shape[1]
    block = lambda w: pl.BlockSpec((qlen, w), lambda i, *_: (i, 0))
    hbm = pl.BlockSpec(memory_space=pl.ANY)
    return pl.pallas_call(
        functools.partial(attention_kernel, len(sources)),
        out_shape=(
            jax.ShapeDtypeStruct((rows, width), BF),
            jax.ShapeDtypeStruct((rows, local), BF),
            jax.ShapeDtypeStruct((slots, PLEN, local), BF),
        ),
        grid_spec=pltpu.PrefetchScalarGridSpec(
            num_scalar_prefetch=3,
            grid=(n_query,),
            in_specs=[block(width), block(width), block(local)] + [hbm] * len(sources),
            out_specs=(block(width), block(local), hbm),
            scratch_shapes=[
                pltpu.VMEM((2, keys, local), BF),
                pltpu.VMEM((2, retrieved * PLEN, local), BF),
                pltpu.VMEM((width, HD), BF),
                pltpu.VMEM((width, HD), BF),
                pltpu.VMEM((keys, width), BF),
                pltpu.VMEM((keys, width), BF),
                pltpu.SemaphoreType.DMA((2, retrieved)),
                pltpu.SemaphoreType.DMA((2, retrieved)),
            ],
        ),
        compiler_params=pltpu.CompilerParams(vmem_limit_bytes=48 * 2**20),
        cost_estimate=pl.CostEstimate(
            flops=10 * n_query * keys * qlen * width,
            bytes_accessed=8 * rows * width + 4 * n_query * keys * local,
            transcendentals=n_query * keys * width,
        ),
        name="attention",
    )(src_buf, src_row, dst_row, queries, out_grad, query_kv, *sources)


def add_returned_kernel(slot_of, got_ref, out_ref, total):
    total[...] = jnp.zeros_like(total)

    @pl.loop(0, got_ref.shape[0])
    def _(n):
        place = slot_of[n]

        @pl.when(place >= 0)
        def _():
            total[place] += got_ref[n].astype(F32)

    out_ref[...] = total[...].astype(BF)


def add_returned(slot_of, returned, passages):
    shape = (passages,) + returned.shape[1:]
    return pl.pallas_call(
        add_returned_kernel,
        out_shape=jax.ShapeDtypeStruct(shape, BF),
        grid_spec=pltpu.PrefetchScalarGridSpec(
            num_scalar_prefetch=1,
            in_specs=[pl.BlockSpec(memory_space=pltpu.VMEM)],
            out_specs=pl.BlockSpec(memory_space=pltpu.VMEM),
            scratch_shapes=[pltpu.VMEM(shape, F32)],
        ),
        compiler_params=pltpu.CompilerParams(vmem_limit_bytes=32 * 2**20),
        cost_estimate=pl.CostEstimate(
            flops=returned.size, bytes_accessed=2 * returned.size, transcendentals=0
        ),
        name="add_returned",
    )(slot_of, returned)


def requests(source_device, source_slot, owners, capacity):
    flat_device = source_device.reshape(-1)
    flat_slot = source_slot.reshape(-1)
    owner_hits = (flat_device[:, None] == jnp.arange(owners, dtype=jnp.int32)[None, :]).astype(
        jnp.int32
    )
    at = jnp.arange(flat_device.shape[0])
    earlier_same = jnp.logical_and(
        flat_device[:, None] == flat_device[None, :], at[None, :] < at[:, None]
    )
    ranking = jnp.sum(earlier_same.astype(jnp.int32), axis=1)
    slot_hits = (ranking[:, None] == jnp.arange(capacity, dtype=jnp.int32)[None, :]).astype(
        jnp.int32
    )
    placed = owner_hits[:, :, None] * slot_hits[:, None, :]
    table = jnp.sum(placed * (flat_slot + 1)[:, None, None], axis=0) - 1
    return flat_device, flat_slot, ranking, table


def per_device(passage_hidden, kv_weight, queries, query_kv, out_grad, source_device, source_slot):
    owners = lax.axis_size("pas")
    rows_local = passage_hidden.shape[0]
    local_width = query_kv.shape[1]
    passages_here = rows_local // PLEN
    queries_here = source_device.shape[0]
    requests_total = queries_here * source_device.shape[1]
    capacity = min(queries_here, max(2, 2 * requests_total // owners))
    flat_device, flat_slot, ranking, table = requests(
        source_device, source_slot, owners, capacity
    )
    wanted = lax.all_to_all(table, "pas", split_axis=0, concat_axis=0, tiled=True)
    partial_kv = jnp.einsum(
        "rd,cd->rc",
        passage_hidden,
        lax.all_gather(kv_weight, "pas", axis=0, tiled=True),
        preferred_element_type=F32,
    )
    passage_kv = lax.psum_scatter(partial_kv, "tp", scatter_dimension=1, tiled=True).astype(BF)
    passage_kv = passage_kv.reshape(passages_here, PLEN, local_width)
    piece_rows = lax.all_gather(passage_kv, "pas", axis=0, tiled=True)
    grad_queries, own_grads, outgoing = attention(
        queries,
        out_grad,
        query_kv,
        [piece_rows],
        jnp.zeros_like(flat_device),
        flat_device * passages_here + flat_slot,
        flat_device * capacity + ranking,
        owners * capacity,
        queries_here,
    )
    returned = lax.all_to_all(outgoing, "pas", split_axis=0, concat_axis=0, tiled=True)
    grad_kv = add_returned(wanted.reshape(-1), returned, passages_here)
    full_grad = lax.all_gather(grad_kv.reshape(rows_local, local_width), "tp", axis=1, tiled=True)
    weight_grad = lax.psum_scatter(
        jnp.einsum("rc,rd->cd", full_grad, passage_hidden, preferred_element_type=F32),
        "pas",
        scatter_dimension=0,
        tiled=True,
    )
    return grad_queries, own_grads, weight_grad


def solution(mesh):
    in_specs = (
        P("pas", "tp"),
        P("pas", "tp"),
        P("pas", "tp"),
        P("pas", "tp"),
        P("pas", "tp"),
        P("pas", None),
        P("pas", None),
    )
    out_specs = (P("pas", "tp"), P("pas", "tp"), P("pas", "tp"))
    return jax.shard_map(
        per_device, mesh=mesh, in_specs=in_specs, out_specs=out_specs, check_vma=False
    )
```

time: 484 us -> 425 us (0.88)
  local copies, waits for them, and re-layouts: 50.2 us -> 1.5 us
  matrix products: 50 us -> 20.6 us
  Pallas kernels: 0 us -> 28.7 us
  other arithmetic: 11.3 us -> 3.12 us
    dot_general x25 -> x0, matrix products: 29.4 us -> none  [the longest x4 5.9 us: attend_block(): jnp.einsum('qhgd,khd->hgqk', grad_heads, value_heads, preferred_element_t...]
    pallas_call x0 -> x2, Pallas kernels: none -> 28.7 us  [the longest x1 23.9 us: attention(): pl.pallas_call(functools.partial(attention_kernel, len(sources)), out_sha...]
    dynamic_slice x28 -> x0, local copies, waits for them, and re-layouts: 14.6 us -> none  [per_device(): lax.map(one_query, (queries.reshape(queries_here, query_length, queries.s...]
    scatter x2 -> x0, local copies, waits for them, and re-layouts: 14.3 us -> none  [per_device(): outgoing_grads.at[flat_device, ranking]]
    dynamic_update_slice x24 -> x0, local copies, waits for them, and re-layouts: 7.83 us -> none  [per_device(): lax.map(one_query, (queries.reshape(queries_here, query_length, queries.s...]
    gather x1 -> x0, local copies, waits for them, and re-layouts: 6.45 us -> none  [per_device(): taken_rows = piece_rows[jnp.clip(global_ids, 0, piece_rows.shape[0] - 1)]]
  transfers between devices with their start and end apart: 7 -> 7, of which waited for: 6 -> 6; matrix products, arithmetic and copies ran while one was open for 17% -> 1% of each run, Pallas kernels for 0% -> 6%
where the time goes in v1:
time: 425 us; the launch traced here: 424 us
  waiting for transfers between devices  343 us (81%)
  Pallas kernels  28.7 us (7%)
  matrix products  20.6 us (5%)
  between operations  13.9 us (3%)
  starting transfers between devices  13.1 us (3%)
    reduce_scatter x1, waiting for transfers between devices, per_device(): lax.psum_scatter(jnp.einsum('rc,rd->cd', full_grad, passage_hidden, prefe...  94 us
    all_gather x1, waiting for transfers between devices, per_device(): piece_rows = lax.all_gather(passage_kv, 'pas', axis=0, tiled=True)  64.9 us
    all_to_all x1, waiting for transfers between devices, per_device(): lax.all_to_all(outgoing, 'pas', split_axis=0, concat_axis=0, tiled=True)  51.4 us
    all_gather x1, waiting for transfers between devices, per_device(): lax.all_gather(kv_weight, 'pas', axis=0, tiled=True)  51.2 us
    reduce_scatter x1, waiting for transfers between devices, per_device(): lax.psum_scatter(partial_kv, 'tp', scatter_dimension=1, tiled=True)  46.2 us
    all_gather x1, waiting for transfers between devices, per_device(): lax.all_gather(grad_kv.reshape(rows_local, local_width), 'tp', axis=1, ti...  34.9 us
    pallas_call x1, Pallas kernels, attention(): pl.pallas_call(functools.partial(attention_kernel, len(sources)), out_sha...  23.9 us
    dot_general x1, matrix products, per_device(): jnp.einsum('rc,rd->cd', full_grad, passage_hidden, preferred_element_type...  10.6 us
  transfers between devices with their start and end apart: 7, of which 6 were waited for; matrix products, arithmetic and copies ran while one was open for 1% of the time, Pallas kernels for 6%

profile of v1, /device:TPU:0, one launch (start us, length us, event | category | flops | bytes accessed | tf_op | source)
XLA Modules:
  0.0 424.2 jit_solution(838210058384062929)
XLA Ops:
  7.2 0.0 all-gather.4.cloned.1.call-start
  7.2 0.7 all-gather.4.cloned.1.call-update
  7.9 0.0 reduce-scatter.3.cloned.1.call-start
  7.9 51.2 %all-gather.4.cloned.1.call-done = bf16[1024,2048]{1,0:T(8,128)(2,1)} async-done(((bf16[32,2048]{1,0:T(8,128)(2,1)}), bf16[1024,2048]{1,0:T(8,128)(2,1)}) %all-gather.4.cloned.1.call-update) | async-done | bytes 4194320 | tf_op jit(solution)/shard_map/all_gather | solution.py:226
  59.2 9.9 %fusion.2 = f32[1024,1024]{1,0:T(8,128)} fusion(bf16[1024,2048]{1,0:T(8,128)(2,1)} %param.7, bf16[1024,2048]{1,0:T(8,128)(2,1)} %all-gather.4.cloned.1.call-done), kind=kOutput, calls=%fused_computation.11 | convolution fusion | flops 4294967296 | bytes 12582912 | tf_op jit(solution)/shard_map/rd,cd->rc/dot_general | solution.py:223
  69.1 0.0 copy-start.3
  69.1 0.0 copy-start.4
  69.1 0.0 copy-start
  69.1 0.0 copy-start.1
  69.1 0.0 copy-start.2
  69.2 0.0 reduce-scatter.3.cloned.1.call-update
  69.2 0.0 all-gather.6.cloned.1.call-start
  69.2 46.2 %reduce-scatter.3.cloned.1.call-done = f32[1024,256]{1,0:T(8,128)} async-done(((f32[1024,1024]{1,0:T(8,128)}), f32[1024,256]{1,0:T(8,128)}) %reduce-scatter.3.cloned.1.call-update) | async-done | bytes 1048592 | tf_op jit(solution)/shard_map/reduce_scatter | solution.py:229
  115.4 2.1 convert_element_type.21
  117.5 0.0 all-gather.6.cloned.1.call-update
  117.5 0.0 copy-done.3
  117.5 0.1 reshape.82
  117.6 0.0 copy-done.4
  117.6 0.1 reshape.83
  117.7 0.2 convert_reduce_fusion
  117.9 0.1 fusion.1
  117.9 0.1 multiply_reduce_fusion
  118.0 0.7 copy.13
  118.7 7.2 %all-to-all-start = ((s32[32,1,2]{2,1,0:T(1,128)}), s32[32,1,2]{2,1,0:T(1,128)S(1)}, u32[]{:S(2)}, u32[]{:S(2)}) async-start(s32[32,1,2]{2,1,0:T(1,128)} %copy.13), calls=%async_computation.1 | async-start | bytes 32768 | tf_op jit(solution)/shard_map/all_to_all | solution.py:222
  126.0 64.9 %all-gather.6.cloned.1.call-done.rest_0_ = bf16[256,128,256]{2,1,0:T(8,128)(2,1)} async-done(((bf16[8,128,256]{2,1,0:T(8,128)(2,1)}), bf16[256,128,256]{2,1,0:T(8,128)(2,1)}) %all-gather.6.cloned.1.call-update) | async-done | bytes 16777232 | tf_op jit(solution)/shard_map/all_gather | solution.py:231
  190.9 0.0 copy-done
  190.9 0.0 copy-done.1
  190.9 0.0 copy-done.2
  190.9 23.9 %attention.1 = (bf16[512,1024]{1,0:T(8,128)(2,1)}, bf16[512,256]{1,0:T(8,128)(2,1)}, bf16[64,128,256]{2,1,0:T(8,128)(2,1)}) custom-call(s32[32]{0:T(128)S(1)} %broadcast_in_dim.2.src_buf, s32[32]{0:T(128)S(1)} %get-tuple-element.10.src_row, s32[32]{0:T(128)S(1)} %get-tuple-element.11.dst_row, bf16[512,1024]{1,0:T(8,128)(2,1)S(1)} %copy-done, ...), custom_call_target="tpu_custom_call" | custom-call | flops 6039797760 | bytes 8912896 | tf_op jit(solution)/shard_map/attention/pallas_call | solution.py:126
  214.8 0.0 all-to-all-done
  214.8 5.5 %all-to-all-start.1 = ((bf16[64,128,256]{2,1,0:T(8,128)(2,1)}), bf16[64,128,256]{2,1,0:T(8,128)(2,1)}, u32[]{:S(2)}, u32[]{:S(2)}) async-start(bf16[64,128,256]{2,1,0:T(8,128)(2,1)} %get-tuple-element.8), calls=%async_computation.2 | async-start | bytes 8388608 | tf_op jit(solution)/shard_map/all_to_all | solution.py:243
  220.3 0.0 all-gather.8.cloned.1.call-start
  220.4 0.5 broadcast.43
  220.9 0.7 reduce.3
  221.6 0.1 reshape.85.slot_of
  221.7 51.4 %all-to-all-done.1.got_ref = bf16[64,128,256]{2,1,0:T(8,128)(2,1)} async-done(((bf16[64,128,256]{2,1,0:T(8,128)(2,1)}), bf16[64,128,256]{2,1,0:T(8,128)(2,1)}, u32[]{:S(2)}, u32[]{:S(2)}) %all-to-all-start.1) | async-done | bytes 4194336 | tf_op jit(solution)/shard_map/all_to_all | solution.py:243
  273.1 4.8 %add_returned.1 = bf16[8,128,256]{2,1,0:T(8,128)(2,1)} custom-call(s32[64]{0:T(128)S(1)} %reshape.85.slot_of, bf16[64,128,256]{2,1,0:T(8,128)(2,1)} %all-to-all-done.1.got_ref), custom_call_target="tpu_custom_call" | custom-call | flops 2097152 | bytes 4194304 | tf_op jit(solution)/shard_map/add_returned/pallas_call | solution.py:175
  277.9 0.0 all-gather.8.cloned.1.call-update
  277.9 0.2 reduce-scatter.5.cloned.1.call-start
  278.2 34.9 %all-gather.8.cloned.1.call-done = bf16[1024,1024]{1,0:T(8,128)(2,1)} async-done(((bf16[1024,256]{1,0:T(8,128)(2,1)}), bf16[1024,1024]{1,0:T(8,128)(2,1)}) %all-gather.8.cloned.1.call-update) | async-done | bytes 2097168 | tf_op jit(solution)/shard_map/all_gather | solution.py:245
  313.0 10.6 %fusion.3 = f32[1024,2048]{1,0:T(8,128)} fusion(bf16[1024,1024]{1,0:T(8,128)(2,1)} %all-gather.8.cloned.1.call-done, bf16[1024,2048]{1,0:T(8,128)(2,1)} %param.7), kind=kOutput, calls=%fused_computation.12 | convolution fusion | flops 4294967296 | bytes 14680064 | tf_op jit(solution)/shard_map/rc,rd->cd/dot_general | solution.py:247
  323.6 0.0 reduce-scatter.5.cloned.1.call-update
  323.7 94.0 %reduce-scatter.5.cloned.1.call-done = f32[32,2048]{1,0:T(8,128)} async-done(((f32[1024,2048]{1,0:T(8,128)}), f32[32,2048]{1,0:T(8,128)}) %reduce-scatter.5.cloned.1.call-update) | async-done | bytes 262160 | tf_op jit(solution)/shard_map/reduce_scatter | solution.py:246
  (4 shorter events, 0.0 us)
Async XLA Ops:
  7.2 52.0 %all-gather.4.cloned.1.call-start = ((), (), s32[]{:S(2)}) async-start(), calls=%async_computation.4 | async-start | bytes 4325376 | tf_op jit(solution)/shard_map/all_gather | solution.py:226
  7.9 107.5 %reduce-scatter.3.cloned.1.call-start = ((), (), s32[]{:S(2)}) async-start(), calls=%async_computation.5 | async-start | bytes 5242880 | tf_op jit(solution)/shard_map/reduce_scatter | solution.py:229
  69.1 48.4 %copy-start.3 = (s32[4,8]{1,0:T(4,128)S(1)}, s32[4,8]{1,0:T(4,128)}, u32[]{:S(2)}) copy-start(s32[4,8]{1,0:T(4,128)} %param.12) | copy-start | bytes 388
  69.1 48.4 %copy-start.4 = (s32[4,8]{1,0:T(4,128)S(1)}, s32[4,8]{1,0:T(4,128)}, u32[]{:S(2)}) copy-start(s32[4,8]{1,0:T(4,128)} %param.13) | copy-start | bytes 388
  69.1 121.7 %copy-start = (bf16[512,1024]{1,0:T(8,128)(2,1)S(1)}, bf16[512,1024]{1,0:T(8,128)(2,1)}, u32[]{:S(2)}) copy-start(bf16[512,1024]{1,0:T(8,128)(2,1)} %q_ref.1) | copy-start | bytes 3145732
  69.1 121.7 %copy-start.1 = (bf16[512,1024]{1,0:T(8,128)(2,1)S(1)}, bf16[512,1024]{1,0:T(8,128)(2,1)}, u32[]{:S(2)}) copy-start(bf16[512,1024]{1,0:T(8,128)(2,1)} %do_ref.1) | copy-start | bytes 3145732
  69.1 121.7 %copy-start.2 = (bf16[512,256]{1,0:T(8,128)(2,1)S(1)}, bf16[512,256]{1,0:T(8,128)(2,1)}, u32[]{:S(2)}) copy-start(bf16[512,256]{1,0:T(8,128)(2,1)} %own_ref.1) | copy-start | bytes 786436
  69.2 121.7 %all-gather.6.cloned.1.call-start = ((), (), s32[]{:S(2)}) async-start(), calls=%async_computation.6 | async-start | bytes 17301504 | tf_op jit(solution)/shard_map/all_gather | solution.py:231
  118.7 96.1 %all-to-all-start = ((s32[32,1,2]{2,1,0:T(1,128)}), s32[32,1,2]{2,1,0:T(1,128)S(1)}, u32[]{:S(2)}, u32[]{:S(2)}) async-start(s32[32,1,2]{2,1,0:T(1,128)} %copy.13), calls=%async_computation.1 | async-start | bytes 32768 | tf_op jit(solution)/shard_map/all_to_all | solution.py:222
  214.8 58.3 %all-to-all-start.1 = ((bf16[64,128,256]{2,1,0:T(8,128)(2,1)}), bf16[64,128,256]{2,1,0:T(8,128)(2,1)}, u32[]{:S(2)}, u32[]{:S(2)}) async-start(bf16[64,128,256]{2,1,0:T(8,128)(2,1)} %get-tuple-element.8), calls=%async_computation.2 | async-start | bytes 8388608 | tf_op jit(solution)/shard_map/all_to_all | solution.py:243
  220.3 92.7 %all-gather.8.cloned.1.call-start = ((), (), s32[]{:S(2)}) async-start(), calls=%async_computation.7 | async-start | bytes 2621440 | tf_op jit(solution)/shard_map/all_gather | solution.py:245
  277.9 139.7 %reduce-scatter.5.cloned.1.call-start = ((), (), s32[]{:S(2)}) async-start(), calls=%async_computation.8 | async-start | bytes 8650752 | tf_op jit(solution)/shard_map/reduce_scatter | solution.py:246
Sparse Core Ops, SparseCore 0:
  10.3 48.8 all-gather.3
  69.3 46.0 reduce-scatter.2
  118.5 72.3 all-gather.5
  278.1 34.9 all-gather.7
  323.8 93.8 reduce-scatter.4
